TPU v7x, 512 devices: a whole 4x4x16 slice. The times are simulated.
512 devices in a mesh: grp: 16 (over y, x_lo, core), blk: 32 (over x_hi, z).
Axes of the slice: x: 4 (x_hi: 2, x_lo: 2; x = x_hi * 2 + x_lo), y: 4, z: 16, core: 2. Of those that a mesh axis runs over, the one named last changes fastest.
Arguments:
- src_emb: float32 [400, 65536], P(None, ('grp', 'blk')), may hold values from -1.5 to 1.5
- src_state: float32 [65536], P(('grp', 'blk')), may hold values from 0.01 to 1
- dst_emb: float32 [400, 65536], P(None, ('grp', 'blk')), may hold values from -1.5 to 1.5
- dst_state: float32 [65536], P(('grp', 'blk')), may hold values from 0.01 to 1
- relations: float32 [8, 400], replicated, may hold values from 0.1 to 1.9
- rel_state: float32 [8], replicated, may hold values from 100 to 10000
- src_ids: int32 [4096, 128], P(('grp', 'blk')), may hold values from 0 to 127
- dst_ids: int32 [4096, 128], P(('grp', 'blk')), may hold values from 0 to 127
- rel_ids: int32 [4096, 128], P(('grp', 'blk')), may hold values from 0 to 7
- neg_ids: int32 [4096, 64], P(('grp', 'blk')), may hold values from 0 to 127
- lengths: int32 [4096], P(('grp', 'blk')), may hold values from 16 to 128, as said below
Outputs:
- src_out: float32 [400, 65536], P(None, ('grp', 'blk'))
- src_state_out: float32 [65536], P(('grp', 'blk'))
- dst_out: float32 [400, 65536], P(None, ('grp', 'blk'))
- dst_state_out: float32 [65536], P(('grp', 'blk'))
- relations_out: float32 [8, 400], replicated
Inputs may be any that keep to these rules, and one draw needn't show every extreme that they name: `lengths`: slots at or beyond a bucket's length are padding; some bucket of every draw is full, and each length is at least 16.
All inputs are finite; a program needn't handle non-finite values.
Results may differ from a plain program's by a relative error of at most 0.0003.
Values sent between devices are 32-bit elements; how exact they have to be, the bound alone decides.
A program may use at most 64 MiB of HBM per device.

v0:
```python
import jax
import jax.numpy as jnp
from jax import lax
from jax.experimental import pallas as pl
from jax.experimental.pallas import tpu as pltpu
from jax.sharding import PartitionSpec as P

learn_rate = 0.1
rel_rate = 0.5
epsilon = 1e-08

D = 400
NREL = 8
ROWS = 128
NEG = 64
ROUNDS = 8
N_GRP = 16
N_BLK = 32
Z = 16

CHUNKS = ((0, 128), (128, 128), (256, 144))
NC = len(CHUNKS)
STATE = D
MOVED = D + 8
MESH = pl.DeviceIdType.MESH
f32, bf16 = jnp.float32, jnp.bfloat16


def halves(x):
    hi = x.astype(bf16)
    return hi, (x - hi.astype(f32)).astype(bf16)


def nn(a, b):
    return lax.dot_general(a, b, (((1,), (0,)), ((), ())), preferred_element_type=f32)


def nt(a, b):
    return lax.dot_general(a, b, (((1,), (1,)), ((), ())), preferred_element_type=f32)


def folded(x):
    return x[:, :ROWS] + x[:, ROWS:]


def picked(table, row):
    index = jnp.broadcast_to(row, table.shape)
    return jnp.take_along_axis(table, index, axis=1, mode="promise_in_bounds")


def sub_iota():
    return lax.broadcasted_iota(jnp.int32, (ROWS, ROWS), 0)


def window(
    lengths,
    rel_state,
    src_e,
    src_s,
    dst_e,
    dst_s,
    rel,
    s_ids,
    d_ids,
    r_ids,
    n_ids,
    src_o,
    src_so,
    dst_o,
    dst_so,
    rel_o,
    mov,
    back,
    w_buf,
    s_buf,
    fixed_t,
    a2,
    d2,
    rel_t,
    rg,
    c1,
    dv,
    packed,
    gotten,
    tiles,
    r1,
    r2,
    r3,
    r4,
    r5,
    send_sem,
    recv_sem,
    back_sem,
    id_send,
    id_recv,
    ar_send,
    ar_recv,
):
    g, b = lax.axis_index("grp"), lax.axis_index("blk")
    y, x_lo, core = g // 4, (g // 2) % 2, g % 2
    x_hi, z = b // Z, b % Z

    def blk(by):
        return (b + by + N_BLK) % N_BLK

    def y_peer(i):
        q = (y + i) % 4
        return q, (q * 4 + x_lo * 2 + core, b)

    def xc_peer(i):
        q = (x_hi * 4 + x_lo * 2 + core + i) % 8
        return q, (y * 4 + q % 4, (q // 4) * Z + z)

    def zl_peer(i):
        q = (z % 4 + i) % 4
        return q, (g, x_hi * Z + (z // 4) * 4 + q)

    def zh_peer(i):
        q = (z // 4 + i) % 4
        return q, (g, x_hi * Z + q * 4 + z % 4)

    stages = ((y_peer, 4), (xc_peer, 8), (zl_peer, 4), (zh_peer, 4))

    barrier = pltpu.get_barrier_semaphore()

    def greet(device):
        pl.semaphore_signal(barrier, inc=1, device_id=device, device_id_type=MESH)

    for peer, n in stages:
        for i in range(1, n):
            greet(peer(i)[1])
    n_peers = sum(n - 1 for _, n in stages)

    for k in range(ROUNDS):
        packed[k, 0:1, :] = s_ids[k : k + 1, :]
        packed[k, 1:2, :] = d_ids[k : k + 1, :]
        packed[k, 2:3, :] = r_ids[k : k + 1, :]
        packed[k, 3:4, :] = jnp.concatenate([n_ids[k : k + 1, :], jnp.full((1, ROWS - NEG), -1, jnp.int32)], axis=1)
        packed[k, 4:8, :] = jnp.full((4, ROWS), lengths[k], jnp.int32)

    wide = jnp.concatenate([rel[...], jnp.zeros((NREL, 512 - D), f32)], axis=1)
    wide = jnp.concatenate([wide, jnp.zeros((ROWS - NREL, 512), f32)], axis=0)
    rel_t[...] = wide.T[:D, :]
    rg[...] = jnp.zeros_like(rg)

    def moved_copy(k, c, device):
        rows = pl.ds(CHUNKS[c][0], CHUNKS[c][1] + (8 if c == NC - 1 else 0))
        return pltpu.make_async_remote_copy(
            src_ref=mov.at[k, rows],
            dst_ref=mov.at[jnp.minimum(k + 1, ROUNDS - 1), rows],
            send_sem=send_sem.at[k, c],
            recv_sem=recv_sem.at[jnp.minimum(k + 1, ROUNDS - 1), c],
            device_id=device,
            device_id_type=MESH,
        )

    def arrived(k, c):
        rows = pl.ds(CHUNKS[c][0], CHUNKS[c][1] + (8 if c == NC - 1 else 0))
        pltpu.make_async_remote_copy(
            src_ref=mov.at[k, rows],
            dst_ref=mov.at[k, rows],
            send_sem=send_sem.at[k, c],
            recv_sem=recv_sem.at[k, c],
            device_id=(g, blk(1)),
            device_id_type=MESH,
        ).wait_recv()

    def home_copy(c, out, device):
        rows = pl.ds(*CHUNKS[c])
        return pltpu.make_async_remote_copy(
            src_ref=mov.at[ROUNDS - 1, rows],
            dst_ref=out.at[rows],
            send_sem=send_sem.at[ROUNDS - 1, c],
            recv_sem=back_sem.at[c],
            device_id=device,
            device_id_type=MESH,
        )

    def home_state_copy(device):
        return pltpu.make_async_remote_copy(
            src_ref=mov.at[ROUNDS - 1, pl.ds(STATE, 8)],
            dst_ref=back,
            send_sem=send_sem.at[ROUNDS - 1, NC],
            recv_sem=back_sem.at[NC],
            device_id=device,
            device_id_type=MESH,
        )

    def stepped(k, grad, out, next_device, home_device):
        state = mov[k, STATE : STATE + 8, :] + jnp.sum(grad * grad, axis=0, keepdims=True) * (1.0 / D)
        scale = (learn_rate / (jnp.sqrt(state) + epsilon))[0:1]
        mov[k, STATE : STATE + 8, :] = state
        for c, (r0, n) in enumerate(CHUNKS):
            mov[k, r0 : r0 + n, :] = mov[k, r0 : r0 + n, :] - grad[r0 : r0 + n] * scale

            @pl.when(k < ROUNDS - 1)
            def _():
                moved_copy(k, c, next_device).start()

            @pl.when(k == ROUNDS - 1)
            def _():
                home_copy(c, out, home_device).start()
                if c == NC - 1:
                    home_state_copy(home_device).start()

    def settled(table, state, grad):
        new = state[...] + jnp.sum(grad * grad, axis=0, keepdims=True) * (1.0 / D)
        state[...] = new
        table[...] = table[...] - grad * (learn_rate / (jnp.sqrt(new) + epsilon))

    def coefficients(tile):
        rows = sub_iota()
        valid = (lax.broadcasted_iota(jnp.int32, (1, ROWS), 1) < tile[4:5]).astype(f32)
        hit = (rows == tile[1:2]).astype(f32)
        count = jnp.sum((rows == tile[3:4]).astype(f32), axis=1, keepdims=True)
        return (count + hit) * valid, hit * valid

    def one_hot2(row):
        hot = (sub_iota() == row).astype(f32).astype(bf16)
        return jnp.concatenate([hot, hot], axis=1)

    def quadrants(x):
        return (x[:ROWS, :ROWS] + x[ROWS:, ROWS:]) + (x[:ROWS, ROWS:] + x[ROWS:, :ROWS])

    def two_by_two(hi, lo):
        line = jnp.concatenate([hi, lo], axis=1)
        return jnp.concatenate([line, line], axis=0)

    def two_by_two_t(hi, lo):
        return jnp.concatenate([jnp.concatenate([hi, hi], axis=1), jnp.concatenate([lo, lo], axis=1)], axis=0)

    def split_into(ref, r0, n, x):
        hi, lo = halves(x)
        ref[r0 : r0 + n, :ROWS] = hi
        ref[r0 : r0 + n, ROWS:] = lo

    def transposed_into(x):
        hi, lo = halves(x.T)
        fixed_t[:ROWS, :] = hi
        fixed_t[ROWS:, :] = lo

    def both(x):
        return jnp.concatenate(halves(x), axis=1)

    @pl.when(core == 0)
    def _():
        greet((g, blk(-1)))
        greet((g, blk(ROUNDS - 1)))
        src_o[...] = src_e[...]
        src_so[...] = src_s[...]
        mov[0, :D, :] = dst_e[...]
        mov[0, STATE : STATE + 8, :] = jnp.broadcast_to(dst_s[...], (8, ROWS))

        def prepare(k):
            tile = packed[k]
            w = picked(rel_t[...], tile[2:3])
            s = picked(src_o[...], tile[0:1])
            a = s * w
            w_buf[...] = w
            s_buf[...] = s
            split_into(a2, 0, D, a)
            transposed_into(a)
            c, v = coefficients(tile)
            c1[...] = c.T
            dv[...] = v.T

        prepare(0)
        pl.semaphore_wait(barrier, n_peers + 2)

        @pl.loop(0, ROUNDS)
        def _(k):
            total = jnp.zeros((2 * ROWS, 2 * ROWS), f32)
            for c, (r0, n) in enumerate(CHUNKS):

                @pl.when(k > 0)
                def _():
                    arrived(k, c)

                split_into(d2, r0, n, mov[k, r0 : r0 + n, :])
                total = total + nn(fixed_t[:, r0 : r0 + n], d2[r0 : r0 + n, :])
            m = c1[...] * jax.nn.sigmoid(quadrants(total)) - dv[...]
            hi, lo = halves(m)
            stepped(k, folded(nn(a2[...], two_by_two(hi, lo))), dst_o, (g, blk(1)), (g, blk(1 - ROUNDS)))

            h = folded(nt(d2[...], two_by_two_t(hi, lo)))
            tile = packed[k]
            settled(src_o, src_so, nt(both(w_buf[...] * h), one_hot2(tile[0:1])))
            rg[:D, :] = rg[:D, :] + nt(both(s_buf[...] * h), one_hot2(tile[2:3]))

            @pl.when(k < ROUNDS - 1)
            def _():
                prepare(k + 1)

    @pl.when(core == 1)
    def _():
        for k in range(1, ROUNDS):
            greet((g, blk(k)))
        greet((g, blk(1 - ROUNDS)))
        dst_o[...] = dst_e[...]
        dst_so[...] = dst_s[...]
        mov[0, :D, :] = src_e[...]
        mov[0, STATE : STATE + 8, :] = jnp.broadcast_to(src_s[...], (8, ROWS))
        gotten[0] = packed[0]

        def id_copy(k):
            return pltpu.make_async_remote_copy(
                src_ref=packed.at[k],
                dst_ref=gotten.at[k],
                send_sem=id_send.at[k],
                recv_sem=id_recv.at[k],
                device_id=(g, blk(-k)),
                device_id_type=MESH,
            )

        def prepare(k):
            tile = gotten[k]
            w_buf[...] = picked(rel_t[...], tile[2:3])
            d = dst_o[...]
            split_into(d2, 0, D, d)
            transposed_into(d)
            c, v = coefficients(tile)
            c1[...] = c
            dv[...] = v

        prepare(0)
        pl.semaphore_wait(barrier, n_peers + ROUNDS)
        for k in range(1, ROUNDS):
            id_copy(k).start()

        @pl.loop(0, ROUNDS)
        def _(k):
            tile = gotten[k]
            total = jnp.zeros((2 * ROWS, 2 * ROWS), f32)
            for c, (r0, n) in enumerate(CHUNKS):

                @pl.when(k > 0)
                def _():
                    arrived(k, c)

                s = picked(mov[k, r0 : r0 + n, :], tile[0:1])
                s_buf[r0 : r0 + n, :] = s
                split_into(a2, r0, n, s * w_buf[r0 : r0 + n, :])
                total = total + nn(fixed_t[:, r0 : r0 + n], a2[r0 : r0 + n, :])
            m = c1[...] * jax.nn.sigmoid(quadrants(total)) - dv[...]
            hi, lo = halves(m)
            h = folded(nn(d2[...], two_by_two(hi, lo)))
            grad = nt(both(w_buf[...] * h), one_hot2(tile[0:1]))
            stepped(k, grad, src_o, (g, blk(-1)), (g, blk(ROUNDS - 1)))

            rg[:D, :] = rg[:D, :] + nt(both(s_buf[...] * h), one_hot2(tile[2:3]))
            settled(dst_o, dst_so, folded(nt(a2[...], two_by_two_t(hi, lo))))

            @pl.when(k < ROUNDS - 1)
            def _():
                id_copy(k + 1).wait_recv()
                prepare(k + 1)

        for k in range(1, ROUNDS):
            id_copy(k).wait_send()

    summed = rg[...].T[:NREL, :]
    for q in range(4):
        tiles[q] = summed[:, q * ROWS : (q + 1) * ROWS]

    first = 0

    def exchange(stage, peer, n, source, buf):
        def copy(i, slot):
            q, device = peer(i)
            return pltpu.make_async_remote_copy(
                src_ref=source(q),
                dst_ref=buf.at[slot],
                send_sem=ar_send.at[stage, q],
                recv_sem=ar_recv.at[stage, slot],
                device_id=device,
                device_id_type=MESH,
            )

        mine = peer(0)[0]
        for i in range(1, n):
            copy(i, mine).start()
        for i in range(1, n):
            copy(i, peer(i)[0]).wait_recv()
        return lambda: [copy(i, mine).wait_send() for i in range(1, n)]

    def added(buf, n):
        value = buf[0]
        for q in range(1, n):
            value = value + buf[q]
        return value

    r1[y] = tiles[y]
    ends = [exchange(0, y_peer, 4, lambda q: tiles.at[q], r1)]
    value = added(r1, 4)
    for stage, (peer, n), buf in ((1, stages[1], r2), (2, stages[2], r3), (3, stages[3], r4)):
        mine = peer(0)[0]
        buf[mine] = value
        ends.append(exchange(stage, peer, n, lambda q, buf=buf, mine=mine: buf.at[mine], buf))
        value = added(buf, n)
    r5[y] = value
    ends.append(exchange(4, y_peer, 4, lambda q: r5.at[y], r5))

    square = r5[0] * r5[0]
    for q in range(1, 4):
        square = square + r5[q] * r5[q]
    old = jnp.zeros((NREL, 1), f32)
    which = lax.broadcasted_iota(jnp.int32, (NREL, 1), 0)
    for r in range(NREL):
        old = jnp.where(which == r, rel_state[r], old)
    rstate = old + jnp.sum(square, axis=1, keepdims=True) * (1.0 / D)
    scale = rel_rate / (jnp.sqrt(rstate) + epsilon)
    for q in range(4):
        lo, hi = q * ROWS, min(D, (q + 1) * ROWS)
        rel_o[:, lo:hi] = rel[:, lo:hi] - r5[q][:, : hi - lo] * scale

    for end in ends:
        end()

    @pl.loop(0, ROUNDS - 1)
    def _(k):
        for c in range(NC):
            moved_copy(k, c, (g, blk(1))).wait_send()

    def closed(out, state_out):
        for c in range(NC):
            home_copy(c, out, (g, blk(1))).wait_recv()
            home_copy(c, out, (g, blk(1))).wait_send()
        home_state_copy((g, blk(1))).wait_recv()
        home_state_copy((g, blk(1))).wait_send()
        state_out[...] = back[0:1, :]

    @pl.when(core == 0)
    def _():
        closed(dst_o, dst_so)

    @pl.when(core == 1)
    def _():
        closed(src_o, src_so)


def local(src_emb, src_state, dst_emb, dst_state, relations, rel_state, src_ids, dst_ids, rel_ids, neg_ids, lengths):
    vmem, smem = pl.BlockSpec(memory_space=pltpu.VMEM), pl.BlockSpec(memory_space=pltpu.SMEM)
    table, line = jax.ShapeDtypeStruct((D, ROWS), f32), jax.ShapeDtypeStruct((1, ROWS), f32)
    outs = pl.pallas_call(
        window,
        out_shape=[table, line, table, line, jax.ShapeDtypeStruct((NREL, D), f32)],
        in_specs=[smem, smem] + [vmem] * 9,
        out_specs=[vmem] * 5,
        scratch_shapes=[
            pltpu.VMEM((ROUNDS, MOVED, ROWS), f32),
            pltpu.VMEM((8, ROWS), f32),
            pltpu.VMEM((D, ROWS), f32),
            pltpu.VMEM((D, ROWS), f32),
            pltpu.VMEM((2 * ROWS, D), bf16),
            pltpu.VMEM((D, 2 * ROWS), bf16),
            pltpu.VMEM((D, 2 * ROWS), bf16),
            pltpu.VMEM((D, ROWS), f32),
            pltpu.VMEM((512, ROWS), f32),
            pltpu.VMEM((ROWS, ROWS), f32),
            pltpu.VMEM((ROWS, ROWS), f32),
            pltpu.VMEM((ROUNDS, 8, ROWS), jnp.int32),
            pltpu.VMEM((ROUNDS, 8, ROWS), jnp.int32),
            pltpu.VMEM((4, 8, ROWS), f32),
            pltpu.VMEM((4, 8, ROWS), f32),
            pltpu.VMEM((8, 8, ROWS), f32),
            pltpu.VMEM((4, 8, ROWS), f32),
            pltpu.VMEM((4, 8, ROWS), f32),
            pltpu.VMEM((4, 8, ROWS), f32),
            pltpu.SemaphoreType.DMA((ROUNDS, NC + 1)),
            pltpu.SemaphoreType.DMA((ROUNDS, NC)),
            pltpu.SemaphoreType.DMA((NC + 1,)),
            pltpu.SemaphoreType.DMA((ROUNDS,)),
            pltpu.SemaphoreType.DMA((ROUNDS,)),
            pltpu.SemaphoreType.DMA((5, 8)),
            pltpu.SemaphoreType.DMA((5, 8)),
        ],
        compiler_params=pltpu.CompilerParams(
            collective_id=0, has_side_effects=True, vmem_limit_bytes=24 * 1024 * 1024
        ),
    )(
        lengths,
        rel_state,
        src_emb,
        src_state.reshape(1, ROWS),
        dst_emb,
        dst_state.reshape(1, ROWS),
        relations,
        src_ids,
        dst_ids,
        rel_ids,
        neg_ids,
    )
    return (outs[0], outs[1].reshape(ROWS), outs[2], outs[3].reshape(ROWS), outs[4])


def solution(mesh):
    both = ("grp", "blk")
    placed = (
        P(None, both),
        P(both),
        P(None, both),
        P(both),
        P(),
        P(),
        P(both, None),
        P(both, None),
        P(both, None),
        P(both, None),
        P(both),
    )
    return jax.shard_map(
        local,
        mesh=mesh,
        in_specs=placed,
        out_specs=(P(None, both), P(both), P(None, both), P(both), P()),
        check_vma=False,
    )
```

profile of v0, /device:TPU:2, one launch (start us, length us, event | category | flops | bytes accessed | tf_op | source)
XLA Modules:
  0.0 107.7 jit_solution(6686190204420658509)
XLA Ops:
  0.6 0.0 copy-start.10
  0.6 0.0 copy-start.7
  0.7 0.0 copy-start.8
  0.7 0.0 copy-start.9
  0.7 0.6 copy-done.10
  1.3 0.0 copy-done.7
  1.3 0.0 copy-done.8
  1.3 0.0 copy-done.9
  1.3 0.0 copy-start
  1.3 0.9 copy-done
  2.3 0.0 copy-start.1
  2.3 0.9 copy-done.1
  3.2 0.0 copy-start.2
  3.2 0.7 copy-done.2
  3.9 0.0 copy-start.3
  3.9 0.7 copy-done.3
  4.6 0.0 copy-start.4
  4.6 0.7 copy-done.4
  5.3 0.0 copy-start.5
  5.3 0.7 copy-done.5
  6.0 0.0 copy-start.6
  6.0 0.7 copy-done.6
  6.7 98.0 %shard_map.146 = (f32[400,128]{1,0:T(8,128)S(1)}, f32[1,128]{1,0:T(1,128)S(1)}, f32[400,128]{1,0:T(8,128)S(1)}, f32[1,128]{1,0:T(1,128)S(1)}, f32[8,400]{1,0:T(8,128)S(1)}) custom-call(s32[8]{0:T(128)S(1)} %copy-done.7, f32[8]{0:T(128)S(1)} %copy-done.8, f32[400,128]{1,0:T(8,128)S(1)} %copy-done, f32[1,128]{1,0:T(1,128)S(1)} %bitcast.4, ...), custom_call_target="tpu_custom_call" | custom-call | tf_op jit(solution)/shard_map/pallas_call | solution.py:444
  104.7 0.7 copy.21
  105.4 0.5 copy.22
  105.9 0.7 copy.23
  106.6 0.5 copy.24
  107.1 0.6 copy.25
Async XLA Ops:
  0.6 0.7 copy-start.10
  0.6 0.7 copy-start.7
  0.7 0.7 copy-start.8
  0.7 0.7 copy-start.9
  1.3 0.9 copy-start
  2.3 0.9 copy-start.1
  3.2 0.7 copy-start.2
  3.9 0.7 copy-start.3
  4.6 0.7 copy-start.4
  5.3 0.7 copy-start.5
  6.0 0.7 copy-start.6
where the time goes:
time: 108 us
  Pallas kernels  98 us (91%)
  local copies, waits for them, and re-layouts  8.98 us (8%)
    pallas_call x1, Pallas kernels, local(): pl.pallas_call(window, out_shape=[table, line, table, line, jax.ShapeDtyp...  98 us
    unnamed x27, local copies, waits for them, and re-layouts  8.98 us

commit v1 on v0

v1 whole, which is shorter than its diff:
```python
import jax
import jax.numpy as jnp
from jax import lax
from jax.experimental import pallas as pl
from jax.experimental.pallas import tpu as pltpu
from jax.sharding import PartitionSpec as P

learn_rate = 0.1
rel_rate = 0.5
epsilon = 1e-08

D = 400
NREL = 8
ROWS = 128
NEG = 64
ROUNDS = 8
N_GRP = 16
N_BLK = 32
Z = 16

CHUNKS = ((0, 128), (128, 128), (256, 144))
NC = len(CHUNKS)
HOME = ((0, 200), (200, 200))
NH = len(HOME)
PART1, PART2, PART3 = (NH,), (0,), (1,)
STATE = D
MOVED = D + 8
MESH = pl.DeviceIdType.MESH
f32, bf16 = jnp.float32, jnp.bfloat16


def halves(x):
    hi = x.astype(bf16)
    return hi, (x - hi.astype(f32)).astype(bf16)


def nn(a, b):
    return lax.dot_general(a, b, (((1,), (0,)), ((), ())), preferred_element_type=f32)


def nt(a, b):
    return lax.dot_general(a, b, (((1,), (1,)), ((), ())), preferred_element_type=f32)


def folded(x):
    return x[:, :ROWS] + x[:, ROWS:]


def picked(table, row):
    index = jnp.broadcast_to(row, table.shape)
    return jnp.take_along_axis(table, index, axis=1, mode="promise_in_bounds")


def sub_iota():
    return lax.broadcasted_iota(jnp.int32, (ROWS, ROWS), 0)


def window(
    lengths_h,
    rel_state_h,
    src_e,
    src_s,
    dst_e,
    dst_s,
    rel_h,
    s_ids_h,
    d_ids_h,
    r_ids_h,
    n_ids_h,
    stay,
    stay_st,
    home,
    home_st,
    rel_o,
    lengths,
    rel_state,
    rel,
    s_ids,
    d_ids,
    r_ids,
    n_ids,
    line,
    mov,
    w_buf,
    s_buf,
    fixed_t,
    a2,
    d2,
    rel_t,
    rg,
    c1,
    dv,
    packed,
    gotten,
    tiles,
    r1,
    r2,
    r3,
    in_sem,
    send_sem,
    recv_sem,
    back_sem,
    id_send,
    id_recv,
    ar_send,
    ar_recv,
):
    g, b = lax.axis_index("grp"), lax.axis_index("blk")
    y, xc, core = g // 4, (b // Z) * 4 + g % 4, g % 2
    x_hi, z = b // Z, b % Z

    small = [
        pltpu.make_async_copy(a, into, in_sem.at[i])
        for i, (a, into) in enumerate(
            (
                (r_ids_h, r_ids),
                (s_ids_h, s_ids),
                (rel_h, rel),
                (d_ids_h, d_ids),
                (n_ids_h, n_ids),
                (lengths_h, lengths),
                (rel_state_h, rel_state),
            )
        )
    ]
    n_small = len(small)

    def tables(keep, keep_st, move, move_st):
        return [
            pltpu.make_async_copy(a, into, in_sem.at[n_small + i])
            for i, (a, into) in enumerate(
                ((keep, stay), (keep_st, stay_st), (move, mov.at[0, pl.ds(0, D)]), (move_st, line))
            )
        ]

    @pl.when(core == 0)
    def _():
        for copy in tables(src_e, src_s, dst_e, dst_s):
            copy.start()

    @pl.when(core == 1)
    def _():
        for copy in tables(dst_e, dst_s, src_e, src_s):
            copy.start()

    for copy in small:
        copy.start()

    def blk(by):
        return (b + by + N_BLK) % N_BLK

    ys = [(y + i) % 4 for i in range(4)]
    xcs = [(xc + i) % 8 for i in range(8)]
    xc_g, xc_b = [q % 4 for q in xcs], [(q // 4) * Z + z for q in xcs]

    def slice_peer(i):
        j, k = i // 8, i % 8
        return ys[j] * 8 + xcs[k], ys[j], (ys[j] * 4 + xc_g[k], xc_b[k])

    def z_peer(i):
        q = (z + i) % Z
        return q, q, (g, x_hi * Z + q)

    def y_peer(i):
        return ys[i], ys[i], (ys[i] * 4 + g % 4, b)

    slice_order = tuple(range(1, 32))
    z_order = (8, 7, 9, 6, 10, 5, 11, 4, 12, 3, 13, 2, 14, 1, 15)
    y_order = (2, 1, 3)
    up = 1 - 2 * core

    barrier = pltpu.get_barrier_semaphore()

    def greet(device):
        pl.semaphore_signal(barrier, inc=1, device_id=device, device_id_type=MESH)

    for i in slice_order:
        greet(slice_peer(i)[2])
    for i in z_order:
        greet(z_peer(i)[2])
    greet((g, blk(-up)))
    greet((g, blk(7 * up)))
    n_peers = len(slice_order) + len(z_order) + 2

    for copy in small:
        copy.wait()

    for k in range(ROUNDS):
        packed[k, 0:1, :] = s_ids[k : k + 1, :]
        packed[k, 1:2, :] = d_ids[k : k + 1, :]
        packed[k, 2:3, :] = r_ids[k : k + 1, :]
        packed[k, 3:4, :] = jnp.concatenate([n_ids[k : k + 1, :], jnp.full((1, ROWS - NEG), -1, jnp.int32)], axis=1)
        packed[k, 4:8, :] = jnp.full((4, ROWS), lengths[k], jnp.int32)

    wide = jnp.concatenate([rel[...], jnp.zeros((NREL, 512 - D), f32)], axis=1)
    wide = jnp.concatenate([wide, jnp.zeros((ROWS - NREL, 512), f32)], axis=0)
    rel_t[...] = wide.T[:D, :]
    for copy in tables(src_e, src_s, dst_e, dst_s):
        copy.wait()
    mov[0, STATE : STATE + 8, :] = jnp.broadcast_to(line[...], (8, ROWS))
    rg[...] = jnp.zeros_like(rg)

    def moved_copy(k, c):
        rows = pl.ds(CHUNKS[c][0], CHUNKS[c][1] + (8 if c == NC - 1 else 0))
        return pltpu.make_async_remote_copy(
            src_ref=mov.at[k, rows],
            dst_ref=mov.at[jnp.minimum(k + 1, ROUNDS - 1), rows],
            send_sem=send_sem.at[k, c],
            recv_sem=recv_sem.at[jnp.minimum(k + 1, ROUNDS - 1), c],
            device_id=(g, blk(up)),
            device_id_type=MESH,
        )

    def arrived(k, c):
        rows = pl.ds(CHUNKS[c][0], CHUNKS[c][1] + (8 if c == NC - 1 else 0))
        pltpu.make_async_remote_copy(
            src_ref=mov.at[k, rows],
            dst_ref=mov.at[k, rows],
            send_sem=send_sem.at[k, c],
            recv_sem=recv_sem.at[k, c],
            device_id=(g, blk(up)),
            device_id_type=MESH,
        ).wait_recv()

    def home_copy(c):
        rows = pl.ds(*HOME[c])
        return pltpu.make_async_remote_copy(
            src_ref=mov.at[ROUNDS - 1, rows],
            dst_ref=home.at[rows],
            send_sem=send_sem.at[ROUNDS - 1, c],
            recv_sem=back_sem.at[c],
            device_id=(g, blk(-7 * up)),
            device_id_type=MESH,
        )

    def home_state_copy():
        return pltpu.make_async_remote_copy(
            src_ref=mov.at[ROUNDS - 1, pl.ds(STATE, 8)],
            dst_ref=home_st,
            send_sem=send_sem.at[ROUNDS - 1, NH],
            recv_sem=back_sem.at[NH],
            device_id=(g, blk(-7 * up)),
            device_id_type=MESH,
        )

    def stepped(k, grad):
        state = mov[k, STATE : STATE + 8, :] + jnp.sum(grad * grad, axis=0, keepdims=True) * (1.0 / D)
        scale = (learn_rate / (jnp.sqrt(state) + epsilon))[0:1]
        mov[k, STATE : STATE + 8, :] = state
        for c, (r0, n) in enumerate(CHUNKS):
            mov[k, r0 : r0 + n, :] = mov[k, r0 : r0 + n, :] - grad[r0 : r0 + n] * scale

            @pl.when(k < ROUNDS - 1)
            def _():
                moved_copy(k, c).start()

    def settled(grad):
        new = stay_st[...] + jnp.sum(grad * grad, axis=0, keepdims=True) * (1.0 / D)
        stay_st[...] = new
        stay[...] = stay[...] - grad * (learn_rate / (jnp.sqrt(new) + epsilon))

    def related(h, tile):
        hot = (lax.broadcasted_iota(jnp.int32, (16, ROWS), 0) == tile[2:3]).astype(f32).astype(bf16)
        rg[:, :D] = rg[:, :D] + nt(jnp.concatenate([hot, hot], axis=1), both(s_buf[...] * h))

    def coefficients(tile):
        rows = sub_iota()
        valid = (lax.broadcasted_iota(jnp.int32, (1, ROWS), 1) < tile[4:5]).astype(f32)
        hit = (rows == tile[1:2]).astype(f32)
        count = jnp.sum((rows == tile[3:4]).astype(f32), axis=1, keepdims=True)
        return (count + hit) * valid, hit * valid

    def one_hot2(row):
        hot = (sub_iota() == row).astype(f32).astype(bf16)
        return jnp.concatenate([hot, hot], axis=1)

    def quadrants(x):
        return (x[:ROWS, :ROWS] + x[ROWS:, ROWS:]) + (x[:ROWS, ROWS:] + x[ROWS:, :ROWS])

    def two_by_two(hi, lo):
        line = jnp.concatenate([hi, lo], axis=1)
        return jnp.concatenate([line, line], axis=0)

    def two_by_two_t(hi, lo):
        return jnp.concatenate([jnp.concatenate([hi, hi], axis=1), jnp.concatenate([lo, lo], axis=1)], axis=0)

    def split_into(ref, r0, n, x):
        hi, lo = halves(x)
        ref[r0 : r0 + n, :ROWS] = hi
        ref[r0 : r0 + n, ROWS:] = lo

    def transposed_into(x):
        hi, lo = halves(x.T)
        fixed_t[:ROWS, :] = hi
        fixed_t[ROWS:, :] = lo

    def both(x):
        return jnp.concatenate(halves(x), axis=1)

    @pl.when(core == 0)
    def _():
        def prepare(k):
            tile = packed[k]
            w = picked(rel_t[...], tile[2:3])
            s = picked(stay[...], tile[0:1])
            a = s * w
            w_buf[...] = w
            s_buf[...] = s
            split_into(a2, 0, D, a)
            transposed_into(a)
            c, v = coefficients(tile)
            c1[...] = c.T
            dv[...] = v.T

        prepare(0)
        pl.semaphore_wait(barrier, n_peers)

        @pl.loop(0, ROUNDS)
        def _(k):
            total = jnp.zeros((2 * ROWS, 2 * ROWS), f32)
            for c, (r0, n) in enumerate(CHUNKS):

                @pl.when(k > 0)
                def _():
                    arrived(k, c)

                split_into(d2, r0, n, mov[k, r0 : r0 + n, :])
                total = total + nn(fixed_t[:, r0 : r0 + n], d2[r0 : r0 + n, :])
            m = c1[...] * jax.nn.sigmoid(quadrants(total)) - dv[...]
            hi, lo = halves(m)
            stepped(k, folded(nn(a2[...], two_by_two(hi, lo))))

            h = folded(nt(d2[...], two_by_two_t(hi, lo)))
            tile = packed[k]
            related(h, tile)
            settled(nt(both(w_buf[...] * h), one_hot2(tile[0:1])))

            @pl.when(k < ROUNDS - 1)
            def _():
                prepare(k + 1)

    @pl.when(core == 1)
    def _():
        for k in range(2, ROUNDS):
            greet((g, blk(k)))
        gotten[0] = packed[0]

        def id_copy(k):
            return pltpu.make_async_remote_copy(
                src_ref=packed.at[k],
                dst_ref=gotten.at[k],
                send_sem=id_send.at[k],
                recv_sem=id_recv.at[k],
                device_id=(g, blk(-k)),
                device_id_type=MESH,
            )

        def prepare(k):
            tile = gotten[k]
            w_buf[...] = picked(rel_t[...], tile[2:3])
            d = stay[...]
            split_into(d2, 0, D, d)
            transposed_into(d)
            c, v = coefficients(tile)
            c1[...] = c
            dv[...] = v

        prepare(0)
        pl.semaphore_wait(barrier, n_peers + ROUNDS - 2)
        for k in range(1, ROUNDS):
            id_copy(k).start()

        @pl.loop(0, ROUNDS)
        def _(k):
            tile = gotten[k]
            total = jnp.zeros((2 * ROWS, 2 * ROWS), f32)
            for c, (r0, n) in enumerate(CHUNKS):

                @pl.when(k > 0)
                def _():
                    arrived(k, c)

                s = picked(mov[k, r0 : r0 + n, :], tile[0:1])
                s_buf[r0 : r0 + n, :] = s
                split_into(a2, r0, n, s * w_buf[r0 : r0 + n, :])
                total = total + nn(fixed_t[:, r0 : r0 + n], a2[r0 : r0 + n, :])
            m = c1[...] * jax.nn.sigmoid(quadrants(total)) - dv[...]
            hi, lo = halves(m)
            h = folded(nn(d2[...], two_by_two(hi, lo)))
            grad = nt(both(w_buf[...] * h), one_hot2(tile[0:1]))
            stepped(k, grad)

            related(h, tile)
            settled(folded(nt(a2[...], two_by_two_t(hi, lo))))

            @pl.when(k < ROUNDS - 1)
            def _():
                id_copy(k + 1).wait_recv()
                prepare(k + 1)

        for k in range(1, ROUNDS):
            id_copy(k).wait_send()

    for q in range(4):
        tiles[q] = rg[:NREL, q * ROWS : (q + 1) * ROWS]

    def exchange(stage, peer, order, source, buf):
        def copy(i, slot):
            _, part, device = peer(i)
            return pltpu.make_async_remote_copy(
                src_ref=source(part),
                dst_ref=buf.at[slot],
                send_sem=ar_send.at[stage, i],
                recv_sem=ar_recv.at[stage, slot],
                device_id=device,
                device_id_type=MESH,
            )

        mine = peer(0)[0]
        for i in order:
            copy(i, mine).start()

        def wait_recv():
            for i in order:
                copy(i, peer(i)[0]).wait_recv()

        def wait_send():
            for i in order:
                copy(i, mine).wait_send()

        return wait_recv, wait_send

    def go_home(parts):
        for c in parts:
            if c == NH:
                home_state_copy().start()
            else:
                home_copy(c).start()

    def added(buf, n):
        value = buf[0]
        for q in range(1, n):
            value = value + buf[q]
        return value

    r1[y * 8 + xc] = tiles[y]
    received, sent1 = exchange(0, slice_peer, slice_order, lambda part: tiles.at[part], r1)
    go_home(PART1)
    received()
    r2[z] = added(r1, 32)
    received, sent2 = exchange(1, z_peer, z_order, lambda part: r2.at[z], r2)
    go_home(PART2)
    received()
    r3[y] = added(r2, Z)
    received, sent3 = exchange(2, y_peer, y_order, lambda part: r3.at[y], r3)
    go_home(PART3)
    received()

    square = r3[0] * r3[0]
    for q in range(1, 4):
        square = square + r3[q] * r3[q]
    old = jnp.zeros((NREL, 1), f32)
    which = lax.broadcasted_iota(jnp.int32, (NREL, 1), 0)
    for r in range(NREL):
        old = jnp.where(which == r, rel_state[r], old)
    rstate = old + jnp.sum(square, axis=1, keepdims=True) * (1.0 / D)
    scale = rel_rate / (jnp.sqrt(rstate) + epsilon)
    for q in range(4):
        lo, hi = q * ROWS, min(D, (q + 1) * ROWS)
        rel_o[:, lo:hi] = rel[:, lo:hi] - r3[q][:, : hi - lo] * scale

    for sent in (sent1, sent2, sent3):
        sent()

    @pl.loop(0, ROUNDS - 1)
    def _(k):
        for c in range(NC):
            moved_copy(k, c).wait_send()

    for c in range(NH):
        home_copy(c).wait_send()
    home_state_copy().wait_send()
    for c in range(NH):
        home_copy(c).wait_recv()
    home_state_copy().wait_recv()


def placed_back(stay, stay_st, home, home_st, rel_v, src_o, src_so, dst_o, dst_so, rel_o, sem):
    def copies(keep, keep_st, move, move_st):
        return [
            pltpu.make_async_copy(a, into, sem.at[i])
            for i, (a, into) in enumerate(
                (
                    (stay, keep),
                    (home, move),
                    (stay_st, keep_st),
                    (home_st.at[pl.ds(0, 1)], move_st),
                    (rel_v, rel_o),
                )
            )
        ]

    core = lax.axis_index("grp") % 2

    @pl.when(core == 0)
    def _():
        for copy in copies(src_o, src_so, dst_o, dst_so):
            copy.start()

    @pl.when(core == 1)
    def _():
        for copy in copies(dst_o, dst_so, src_o, src_so):
            copy.start()

    for copy in copies(src_o, src_so, dst_o, dst_so):
        copy.wait()


def local(src_emb, src_state, dst_emb, dst_state, relations, rel_state, src_ids, dst_ids, rel_ids, neg_ids, lengths):
    vmem, hbm = pl.BlockSpec(memory_space=pltpu.VMEM), pl.BlockSpec(memory_space=pltpu.HBM)
    table, line = jax.ShapeDtypeStruct((D, ROWS), f32), jax.ShapeDtypeStruct((1, ROWS), f32)
    relation = jax.ShapeDtypeStruct((NREL, D), f32)
    ids = pltpu.VMEM((ROUNDS, ROWS), jnp.int32)
    results = pl.pallas_call(
        window,
        out_shape=[table, line, table, jax.ShapeDtypeStruct((8, ROWS), f32), relation],
        in_specs=[hbm] * 11,
        out_specs=[vmem] * 5,
        scratch_shapes=[
            pltpu.SMEM((ROUNDS,), jnp.int32),
            pltpu.SMEM((NREL,), f32),
            pltpu.VMEM((NREL, D), f32),
            ids,
            ids,
            ids,
            pltpu.VMEM((ROUNDS, NEG), jnp.int32),
            pltpu.VMEM((1, ROWS), f32),
            pltpu.VMEM((ROUNDS, MOVED, ROWS), f32),
            pltpu.VMEM((D, ROWS), f32),
            pltpu.VMEM((D, ROWS), f32),
            pltpu.VMEM((2 * ROWS, D), bf16),
            pltpu.VMEM((D, 2 * ROWS), bf16),
            pltpu.VMEM((D, 2 * ROWS), bf16),
            pltpu.VMEM((D, ROWS), f32),
            pltpu.VMEM((16, 512), f32),
            pltpu.VMEM((ROWS, ROWS), f32),
            pltpu.VMEM((ROWS, ROWS), f32),
            pltpu.VMEM((ROUNDS, 8, ROWS), jnp.int32),
            pltpu.VMEM((ROUNDS, 8, ROWS), jnp.int32),
            pltpu.VMEM((4, 8, ROWS), f32),
            pltpu.VMEM((32, 8, ROWS), f32),
            pltpu.VMEM((Z, 8, ROWS), f32),
            pltpu.VMEM((4, 8, ROWS), f32),
            pltpu.SemaphoreType.DMA((11,)),
            pltpu.SemaphoreType.DMA((ROUNDS, max(NC, NH + 1))),
            pltpu.SemaphoreType.DMA((ROUNDS, NC)),
            pltpu.SemaphoreType.DMA((NH + 1,)),
            pltpu.SemaphoreType.DMA((ROUNDS,)),
            pltpu.SemaphoreType.DMA((ROUNDS,)),
            pltpu.SemaphoreType.DMA((3, 32)),
            pltpu.SemaphoreType.DMA((3, 32)),
        ],
        compiler_params=pltpu.CompilerParams(
            collective_id=0, has_side_effects=True, vmem_limit_bytes=60 * 1024 * 1024
        ),
    )(
        lengths,
        rel_state,
        src_emb,
        src_state.reshape(1, ROWS),
        dst_emb,
        dst_state.reshape(1, ROWS),
        relations,
        src_ids,
        dst_ids,
        rel_ids,
        neg_ids,
    )
    outs = pl.pallas_call(
        placed_back,
        out_shape=[table, line, table, line, relation],
        in_specs=[vmem] * 5,
        out_specs=[hbm] * 5,
        scratch_shapes=[pltpu.SemaphoreType.DMA((5,))],
    )(*results)
    return (outs[0], outs[1].reshape(ROWS), outs[2], outs[3].reshape(ROWS), outs[4])


def solution(mesh):
    both = ("grp", "blk")
    placed = (
        P(None, both),
        P(both),
        P(None, both),
        P(both),
        P(),
        P(),
        P(both, None),
        P(both, None),
        P(both, None),
        P(both, None),
        P(both),
    )
    return jax.shard_map(
        local,
        mesh=mesh,
        in_specs=placed,
        out_specs=(P(None, both), P(both), P(None, both), P(both), P()),
        check_vma=False,
    )
```

time: 108 us -> 92.8 us (0.86)
  the two profiles are of different devices: /device:TPU:2 before, /device:TPU:7 now
where the time goes in v1:
time: 92.8 us; the launch traced here: 92.7 us
  Pallas kernels  92 us (99%)
    pallas_call x1, Pallas kernels, local(): pl.pallas_call(window, out_shape=[table, line, table, jax.ShapeDtypeStruc...  90.2 us

profile of v1, /device:TPU:7, one launch (start us, length us, event | category | flops | bytes accessed | tf_op | source)
XLA Modules:
  0.0 92.7 jit_solution(6802929163203088803)
XLA Ops:
  0.6 90.2 %shard_map.146 = (f32[400,128]{1,0:T(8,128)}, f32[1,128]{1,0:T(1,128)}, f32[400,128]{1,0:T(8,128)}, f32[8,128]{1,0:T(8,128)}, f32[8,400]{1,0:T(8,128)}) custom-call(s32[8]{0:T(128)} %lengths_h.1, f32[8]{0:T(128)} %rel_state_h.1, f32[400,128]{1,0:T(8,128)} %src_e.1, f32[1,128]{1,0:T(1,128)} %bitcast.4, f32[400,128]{1,0:T(8,128)} %dst_e.1, f32[1,128]{1,0:T(1,128)} %bitcast.5, ...), custom_call_target="tpu_custom_call" | custom-call | tf_op jit(solution)/shard_map/pallas_call | solution.py:524
  90.9 1.8 %shard_map.147 = (f32[400,128]{1,0:T(8,128)}, f32[1,128]{1,0:T(1,128)}, f32[400,128]{1,0:T(8,128)}, f32[1,128]{1,0:T(1,128)}, f32[8,400]{1,0:T(8,128)}) custom-call(f32[400,128]{1,0:T(8,128)} %get-tuple-element.15.stay, f32[1,128]{1,0:T(1,128)} %get-tuple-element.16.stay_st, f32[400,128]{1,0:T(8,128)} %get-tuple-element.17.home, ...), custom_call_target="tpu_custom_call" | custom-call | tf_op jit(solution)/shard_map/pallas_call | solution.py:579

commit v2 on v1

--- a/solution.py
+++ b/solution.py
@@ -22,7 +22,7 @@
 NC = len(CHUNKS)
 HOME = ((0, 200), (200, 200))
 NH = len(HOME)
-PART1, PART2, PART3 = (NH,), (0,), (1,)
+EARLY, MIDDLE = (0, 3), (3, 16)
 STATE = D
 MOVED = D + 8
 MESH = pl.DeviceIdType.MESH
@@ -109,6 +109,40 @@
     y, xc, core = g // 4, (b // Z) * 4 + g % 4, g % 2
     x_hi, z = b // Z, b % Z
 
+    def blk(by):
+        return (b + by + N_BLK) % N_BLK
+
+    ys = [(y + i) % 4 for i in range(4)]
+    xcs = [(xc + i) % 8 for i in range(8)]
+    xc_g, xc_b = [q % 4 for q in xcs], [(q // 4) * Z + z for q in xcs]
+
+    def slice_peer(i):
+        j, k = i // 8, i % 8
+        return ys[j] * 8 + xcs[k], ys[j], (ys[j] * 4 + xc_g[k], xc_b[k])
+
+    def z_peer(i):
+        q = (z + i) % Z
+        return q, q, (g, x_hi * Z + q)
+
+    def y_peer(i):
+        return ys[i], ys[i], (ys[i] * 4 + g % 4, b)
+
+    slice_order = tuple(range(1, 32))
+    z_order = (8, 7, 9, 6, 10, 5, 11, 4, 12, 3, 13, 2, 14, 1, 15)
+    y_order = (2, 1, 3)
+    up = 1 - 2 * core
+
+    barrier = pltpu.get_barrier_semaphore()
+
+    def greet(device):
+        pl.semaphore_signal(barrier, inc=1, device_id=device, device_id_type=MESH)
+
+    for i in z_order:
+        greet(z_peer(i)[2])
+    for i in slice_order:
+        greet(slice_peer(i)[2])
+    greet((g, blk(-up)))
+    greet((g, blk(7 * up)))
     small = [
         pltpu.make_async_copy(a, into, in_sem.at[i])
         for i, (a, into) in enumerate(
@@ -146,40 +180,6 @@
     for copy in small:
         copy.start()
 
-    def blk(by):
-        return (b + by + N_BLK) % N_BLK
-
-    ys = [(y + i) % 4 for i in range(4)]
-    xcs = [(xc + i) % 8 for i in range(8)]
-    xc_g, xc_b = [q % 4 for q in xcs], [(q // 4) * Z + z for q in xcs]
-
-    def slice_peer(i):
-        j, k = i // 8, i % 8
-        return ys[j] * 8 + xcs[k], ys[j], (ys[j] * 4 + xc_g[k], xc_b[k])
-
-    def z_peer(i):
-        q = (z + i) % Z
-        return q, q, (g, x_hi * Z + q)
-
-    def y_peer(i):
-        return ys[i], ys[i], (ys[i] * 4 + g % 4, b)
-
-    slice_order = tuple(range(1, 32))
-    z_order = (8, 7, 9, 6, 10, 5, 11, 4, 12, 3, 13, 2, 14, 1, 15)
-    y_order = (2, 1, 3)
-    up = 1 - 2 * core
-
-    barrier = pltpu.get_barrier_semaphore()
-
-    def greet(device):
-        pl.semaphore_signal(barrier, inc=1, device_id=device, device_id_type=MESH)
-
-    for i in slice_order:
-        greet(slice_peer(i)[2])
-    for i in z_order:
-        greet(z_peer(i)[2])
-    greet((g, blk(-up)))
-    greet((g, blk(7 * up)))
     n_peers = len(slice_order) + len(z_order) + 2
 
     for copy in small:
@@ -430,11 +430,17 @@
 
         return wait_recv, wait_send
 
-    def go_home(parts):
-        for c in parts:
-            if c == NH:
-                home_state_copy().start()
-            else:
+    home_z = (z + Z - 7 * up) % Z
+
+    def go_home(turn):
+        early = (home_z >= EARLY[0]) & (home_z < EARLY[1])
+        middle = (home_z >= MIDDLE[0]) & (home_z < MIDDLE[1])
+        now = (early, middle, jnp.logical_not(early | middle))[turn]
+
+        @pl.when(now)
+        def _():
+            home_state_copy().start()
+            for c in range(NH):
                 home_copy(c).start()
 
     def added(buf, n):
@@ -445,15 +451,15 @@
 
     r1[y * 8 + xc] = tiles[y]
     received, sent1 = exchange(0, slice_peer, slice_order, lambda part: tiles.at[part], r1)
-    go_home(PART1)
+    go_home(0)
     received()
     r2[z] = added(r1, 32)
     received, sent2 = exchange(1, z_peer, z_order, lambda part: r2.at[z], r2)
-    go_home(PART2)
+    go_home(1)
     received()
     r3[y] = added(r2, Z)
     received, sent3 = exchange(2, y_peer, y_order, lambda part: r3.at[y], r3)
-    go_home(PART3)
+    go_home(2)
     received()
 
     square = r3[0] * r3[0]

time: 92.8 us -> 86 us (0.927)
  the two profiles are of different devices: /device:TPU:7 before, /device:TPU:1 now
where the time goes in v2:
time: 86 us; the launch traced here: 85.8 us
  Pallas kernels  85.2 us (99%)
    pallas_call x1, Pallas kernels, local(): pl.pallas_call(window, out_shape=[table, line, table, jax.ShapeDtypeStruc...  83.4 us
    pallas_call x1, Pallas kernels, local(): pl.pallas_call(placed_back, out_shape=[table, line, table, line, relation...  1.84 us

profile of v2, /device:TPU:1, one launch (start us, length us, event | category | flops | bytes accessed | tf_op | source)
XLA Modules:
  0.0 85.8 jit_solution(16851265297547540151)
XLA Ops:
  0.6 83.4 %shard_map.146 = (f32[400,128]{1,0:T(8,128)}, f32[1,128]{1,0:T(1,128)}, f32[400,128]{1,0:T(8,128)}, f32[8,128]{1,0:T(8,128)}, f32[8,400]{1,0:T(8,128)}) custom-call(s32[8]{0:T(128)} %lengths_h.1, f32[8]{0:T(128)} %rel_state_h.1, f32[400,128]{1,0:T(8,128)} %src_e.1, f32[1,128]{1,0:T(1,128)} %bitcast.4, f32[400,128]{1,0:T(8,128)} %dst_e.1, f32[1,128]{1,0:T(1,128)} %bitcast.5, ...), custom_call_target="tpu_custom_call" | custom-call | tf_op jit(solution)/shard_map/pallas_call | solution.py:530
  84.0 1.8 %shard_map.147 = (f32[400,128]{1,0:T(8,128)}, f32[1,128]{1,0:T(1,128)}, f32[400,128]{1,0:T(8,128)}, f32[1,128]{1,0:T(1,128)}, f32[8,400]{1,0:T(8,128)}) custom-call(f32[400,128]{1,0:T(8,128)} %get-tuple-element.15.stay, f32[1,128]{1,0:T(1,128)} %get-tuple-element.16.stay_st, f32[400,128]{1,0:T(8,128)} %get-tuple-element.17.home, ...), custom_call_target="tpu_custom_call" | custom-call | tf_op jit(solution)/shard_map/pallas_call | solution.py:585

commit v3 on v2

--- a/solution.py
+++ b/solution.py
@@ -86,6 +86,7 @@
     fixed_t,
     a2,
     d2,
+    m2,
     rel_t,
     rg,
     c1,
@@ -127,7 +128,8 @@
     def y_peer(i):
         return ys[i], ys[i], (ys[i] * 4 + g % 4, b)
 
-    slice_order = tuple(range(1, 32))
+    far_y, far_x = (0, 2, 4, 2), (0, 1, 2, 3, 4, 3, 2, 1)
+    slice_order = sorted(range(1, 32), key=lambda i: -(far_y[i // 8] + far_x[i % 8]))
     z_order = (8, 7, 9, 6, 10, 5, 11, 4, 12, 3, 13, 2, 14, 1, 15)
     y_order = (2, 1, 3)
     up = 1 - 2 * core
@@ -249,9 +251,7 @@
         mov[k, STATE : STATE + 8, :] = state
         for c, (r0, n) in enumerate(CHUNKS):
             mov[k, r0 : r0 + n, :] = mov[k, r0 : r0 + n, :] - grad[r0 : r0 + n] * scale
-
-            @pl.when(k < ROUNDS - 1)
-            def _():
+            if not isinstance(k, int):
                 moved_copy(k, c).start()
 
     def settled(grad):
@@ -293,6 +293,11 @@
         hi, lo = halves(x.T)
         fixed_t[:ROWS, :] = hi
         fixed_t[ROWS:, :] = lo
+
+    def left_over(hi, lo, h):
+        m2[:, :ROWS] = hi
+        m2[:, ROWS:] = lo
+        w_buf[...] = w_buf[...] * h
 
     def both(x):
         return jnp.concatenate(halves(x), axis=1)
@@ -328,16 +333,23 @@
                 total = total + nn(fixed_t[:, r0 : r0 + n], d2[r0 : r0 + n, :])
             m = c1[...] * jax.nn.sigmoid(quadrants(total)) - dv[...]
             hi, lo = halves(m)
-            stepped(k, folded(nn(a2[...], two_by_two(hi, lo))))
+
+            @pl.when(k < ROUNDS - 1)
+            def _():
+                stepped(k, folded(nn(a2[...], two_by_two(hi, lo))))
 
             h = folded(nt(d2[...], two_by_two_t(hi, lo)))
             tile = packed[k]
             related(h, tile)
-            settled(nt(both(w_buf[...] * h), one_hot2(tile[0:1])))
 
             @pl.when(k < ROUNDS - 1)
             def _():
+                settled(nt(both(w_buf[...] * h), one_hot2(tile[0:1])))
                 prepare(k + 1)
+
+            @pl.when(k == ROUNDS - 1)
+            def _():
+                left_over(hi, lo, h)
 
     @pl.when(core == 1)
     def _():
@@ -387,16 +399,22 @@
             m = c1[...] * jax.nn.sigmoid(quadrants(total)) - dv[...]
             hi, lo = halves(m)
             h = folded(nn(d2[...], two_by_two(hi, lo)))
-            grad = nt(both(w_buf[...] * h), one_hot2(tile[0:1]))
-            stepped(k, grad)
-
-            related(h, tile)
-            settled(folded(nt(a2[...], two_by_two_t(hi, lo))))
 
             @pl.when(k < ROUNDS - 1)
             def _():
+                stepped(k, nt(both(w_buf[...] * h), one_hot2(tile[0:1])))
+
+            related(h, tile)
+
+            @pl.when(k < ROUNDS - 1)
+            def _():
+                settled(folded(nt(a2[...], two_by_two_t(hi, lo))))
                 id_copy(k + 1).wait_recv()
                 prepare(k + 1)
+
+            @pl.when(k == ROUNDS - 1)
+            def _():
+                left_over(hi, lo, h)
 
         for k in range(1, ROUNDS):
             id_copy(k).wait_send()
@@ -451,7 +469,28 @@
 
     r1[y * 8 + xc] = tiles[y]
     received, sent1 = exchange(0, slice_peer, slice_order, lambda part: tiles.at[part], r1)
+
+    hi, lo = m2[:, :ROWS], m2[:, ROWS:]
+    last = ROUNDS - 1
+
+    @pl.when(core == 0)
+    def _():
+        stepped(last, folded(nn(a2[...], two_by_two(hi, lo))))
+
+    @pl.when(core == 1)
+    def _():
+        stepped(last, nt(both(w_buf[...]), one_hot2(gotten[last, 0:1])))
+
     go_home(0)
+
+    @pl.when(core == 0)
+    def _():
+        settled(nt(both(w_buf[...]), one_hot2(packed[last, 0:1])))
+
+    @pl.when(core == 1)
+    def _():
+        settled(folded(nt(a2[...], two_by_two_t(hi, lo))))
+
     received()
     r2[z] = added(r1, 32)
     received, sent2 = exchange(1, z_peer, z_order, lambda part: r2.at[z], r2)
@@ -491,35 +530,40 @@
     home_state_copy().wait_recv()
 
 
-def placed_back(stay, stay_st, home, home_st, rel_v, src_o, src_so, dst_o, dst_so, rel_o, sem):
-    def copies(keep, keep_st, move, move_st):
-        return [
-            pltpu.make_async_copy(a, into, sem.at[i])
-            for i, (a, into) in enumerate(
-                (
-                    (stay, keep),
-                    (home, move),
-                    (stay_st, keep_st),
-                    (home_st.at[pl.ds(0, 1)], move_st),
-                    (rel_v, rel_o),
-                )
-            )
-        ]
+def placed_back(stay_h, stay_st_h, home_h, home_st_h, rel_h, src_o, src_so, dst_o, dst_so, rel_o, *scratch):
+    stay, stay_st, home, home_st, rel_v, in_sem, out_sem = scratch
+    half = D // 2
+    rows = [pl.ds(0, half), pl.ds(half, half)]
+
+    def pieces(a, b, c, d, e):
+        return [a.at[rows[0]], a.at[rows[1]], c.at[rows[0]], c.at[rows[1]], b, d, e]
+
+    held = pieces(stay, stay_st, home, home_st.at[pl.ds(0, 1)], rel_v)
+    came = pieces(stay_h, stay_st_h, home_h, home_st_h.at[pl.ds(0, 1)], rel_h)
+    reads = [pltpu.make_async_copy(a, b, in_sem.at[i]) for i, (a, b) in enumerate(zip(came, held))]
+    for copy in reads:
+        copy.start()
+
+    def writes(keep, keep_st, move, move_st):
+        targets = pieces(keep, keep_st, move, move_st, rel_o)
+        return [pltpu.make_async_copy(a, b, out_sem.at[i]) for i, (a, b) in enumerate(zip(held, targets))]
 
     core = lax.axis_index("grp") % 2
 
     @pl.when(core == 0)
     def _():
-        for copy in copies(src_o, src_so, dst_o, dst_so):
-            copy.start()
+        for read, write in zip(reads, writes(src_o, src_so, dst_o, dst_so)):
+            read.wait()
+            write.start()
 
     @pl.when(core == 1)
     def _():
-        for copy in copies(dst_o, dst_so, src_o, src_so):
-            copy.start()
-
-    for copy in copies(src_o, src_so, dst_o, dst_so):
-        copy.wait()
+        for read, write in zip(reads, writes(dst_o, dst_so, src_o, src_so)):
+            read.wait()
+            write.start()
+
+    for write in writes(src_o, src_so, dst_o, dst_so):
+        write.wait()
 
 
 def local(src_emb, src_state, dst_emb, dst_state, relations, rel_state, src_ids, dst_ids, rel_ids, neg_ids, lengths):
@@ -547,6 +591,7 @@
             pltpu.VMEM((2 * ROWS, D), bf16),
             pltpu.VMEM((D, 2 * ROWS), bf16),
             pltpu.VMEM((D, 2 * ROWS), bf16),
+            pltpu.VMEM((ROWS, 2 * ROWS), bf16),
             pltpu.VMEM((D, ROWS), f32),
             pltpu.VMEM((16, 512), f32),
             pltpu.VMEM((ROWS, ROWS), f32),
@@ -585,9 +630,17 @@
     outs = pl.pallas_call(
         placed_back,
         out_shape=[table, line, table, line, relation],
-        in_specs=[vmem] * 5,
+        in_specs=[hbm] * 5,
         out_specs=[hbm] * 5,
-        scratch_shapes=[pltpu.SemaphoreType.DMA((5,))],
+        scratch_shapes=[
+            pltpu.VMEM((D, ROWS), f32),
+            pltpu.VMEM((1, ROWS), f32),
+            pltpu.VMEM((D, ROWS), f32),
+            pltpu.VMEM((8, ROWS), f32),
+            pltpu.VMEM((NREL, D), f32),
+            pltpu.SemaphoreType.DMA((7,)),
+            pltpu.SemaphoreType.DMA((7,)),
+        ],
     )(*results)
     return (outs[0], outs[1].reshape(ROWS), outs[2], outs[3].reshape(ROWS), outs[4])
 

time: 86 us -> 85.2 us (level)
  the two profiles are of different devices: /device:TPU:1 before, /device:TPU:160 now
where the time goes in v3:
time: 85.2 us; the launch traced here: 85 us
  Pallas kernels  84.4 us (99%)
    pallas_call x1, Pallas kernels, local(): pl.pallas_call(window, out_shape=[table, line, table, jax.ShapeDtypeStruc...  82.6 us
    pallas_call x1, Pallas kernels, local(): pl.pallas_call(placed_back, out_shape=[table, line, table, line, relation...  1.81 us

profile of v3, /device:TPU:160, one launch (start us, length us, event | category | flops | bytes accessed | tf_op | source)
XLA Modules:
  0.0 85.0 jit_solution(1976818978403285031)
XLA Ops:
  0.6 82.6 %shard_map.146 = (f32[400,128]{1,0:T(8,128)}, f32[1,128]{1,0:T(1,128)}, f32[400,128]{1,0:T(8,128)}, f32[8,128]{1,0:T(8,128)}, f32[8,400]{1,0:T(8,128)}) custom-call(s32[8]{0:T(128)} %lengths_h.1, f32[8]{0:T(128)} %rel_state_h.1, f32[400,128]{1,0:T(8,128)} %src_e.1, f32[1,128]{1,0:T(1,128)} %bitcast.4, f32[400,128]{1,0:T(8,128)} %dst_e.1, f32[1,128]{1,0:T(1,128)} %bitcast.5, ...), custom_call_target="tpu_custom_call" | custom-call | tf_op jit(solution)/shard_map/pallas_call | solution.py:574
  83.2 1.8 %shard_map.147 = (f32[400,128]{1,0:T(8,128)}, f32[1,128]{1,0:T(1,128)}, f32[400,128]{1,0:T(8,128)}, f32[1,128]{1,0:T(1,128)}, f32[8,400]{1,0:T(8,128)}) custom-call(f32[400,128]{1,0:T(8,128)} %get-tuple-element.15.stay_h, f32[1,128]{1,0:T(1,128)} %get-tuple-element.16.stay_st_h, f32[400,128]{1,0:T(8,128)} %get-tuple-element.17.home_h, ...), custom_call_target="tpu_custom_call" | custom-call | tf_op jit(solution)/shard_map/pallas_call | solution.py:630

commit v4 on v3

--- a/solution.py
+++ b/solution.py
@@ -18,9 +18,9 @@
 N_BLK = 32
 Z = 16
 
-CHUNKS = ((0, 128), (128, 128), (256, 144))
+CHUNKS = ((0, 128), (128, 128), (256, 128), (384, 16))
 NC = len(CHUNKS)
-HOME = ((0, 200), (200, 200))
+HOME = ((0, 400),)
 NH = len(HOME)
 EARLY, MIDDLE = (0, 3), (3, 16)
 STATE = D

time: 85.2 us -> 85.2 us (level)
  no operation moved by 1% of the time
where the time goes in v4:
time: 85.2 us; the launch traced here: 85 us
  Pallas kernels  84.4 us (99%)
    pallas_call x1, Pallas kernels, local(): pl.pallas_call(window, out_shape=[table, line, table, jax.ShapeDtypeStruc...  82.6 us
    pallas_call x1, Pallas kernels, local(): pl.pallas_call(placed_back, out_shape=[table, line, table, line, relation...  1.81 us

profile of v4, /device:TPU:160, one launch (start us, length us, event | category | flops | bytes accessed | tf_op | source)
XLA Modules:
  0.0 85.0 jit_solution(8931998897193954351)
XLA Ops:
  0.6 82.6 %shard_map.146 = (f32[400,128]{1,0:T(8,128)}, f32[1,128]{1,0:T(1,128)}, f32[400,128]{1,0:T(8,128)}, f32[8,128]{1,0:T(8,128)}, f32[8,400]{1,0:T(8,128)}) custom-call(s32[8]{0:T(128)} %lengths_h.1, f32[8]{0:T(128)} %rel_state_h.1, f32[400,128]{1,0:T(8,128)} %src_e.1, f32[1,128]{1,0:T(1,128)} %bitcast.4, f32[400,128]{1,0:T(8,128)} %dst_e.1, f32[1,128]{1,0:T(1,128)} %bitcast.5, ...), custom_call_target="tpu_custom_call" | custom-call | tf_op jit(solution)/shard_map/pallas_call | solution.py:574
  83.2 1.8 %shard_map.147 = (f32[400,128]{1,0:T(8,128)}, f32[1,128]{1,0:T(1,128)}, f32[400,128]{1,0:T(8,128)}, f32[1,128]{1,0:T(1,128)}, f32[8,400]{1,0:T(8,128)}) custom-call(f32[400,128]{1,0:T(8,128)} %get-tuple-element.15.stay_h, f32[1,128]{1,0:T(1,128)} %get-tuple-element.16.stay_st_h, f32[400,128]{1,0:T(8,128)} %get-tuple-element.17.home_h, ...), custom_call_target="tpu_custom_call" | custom-call | tf_op jit(solution)/shard_map/pallas_call | solution.py:630
